TPU v7x, 32 devices: a whole 2x2x4 slice. The times are simulated.
32 devices in a mesh: dev: 32 (over z, y, x, core).
Axes of the slice: x: 2, y: 2, z: 4, core: 2. Of those that a mesh axis runs over, the one named last changes fastest.
Arguments:
- vectors: bfloat16 [8, 524288], P(None, 'dev'), may hold values from -1.5 to 1.5
- points: float32 [3, 524288], P(None, 'dev'), may hold values from -4 to 4
- leaf_basis: bfloat16 [2048, 64, 256], P('dev'), may hold values from -0.375 to 0.375
- near_list: int32 [2048, 8], P('dev'), may hold values from -32 to 32, as said below
- far_list: int32 [1984, 4], P('dev'), may hold values from -32 to 32, as said below
- transfer: bfloat16 [2016, 64, 128], P('dev'), may hold values from -0.625 to 0.625
- skeleton: float32 [2016, 192], P('dev'), may hold values from -4 to 4
- transfer_top: bfloat16 [31, 64, 128], replicated, may hold values from -0.625 to 0.625
- skeleton_top: float32 [30, 192], replicated, may hold values from -4 to 4
Outputs:
- product: float32 [8, 524288], P(None, 'dev')
Inputs may be any that keep to these rules, and one draw needn't show every extreme that they name: `near_list`: slot 0 of every row holds 0 (the leaf itself); every other slot holds 0 (empty) or a nonzero offset such that the leaf plus the offset is a leaf; the nonzero offsets of a row are distinct. `far_list`: rows follow the numbering of the transfer rows of levels 1 to log2(64) - 1. An entry is 0 (empty) or a nonzero offset of magnitude 2 or more and at most that level's clusters on one device, such that the cluster plus the offset is a cluster of the same level; the nonzero offsets of a row are distinct.
All inputs are finite; a program needn't handle non-finite values.
Results may differ from a plain program's by a relative error of at most 0.002.
Values may be sent and summed in bfloat16 or wider, within the bound.
A program may use at most 64 MiB of HBM per device.

v0:
```python
import jax
import jax.numpy as jnp
from jax import lax
from jax.sharding import PartitionSpec as P

highest = lax.Precision.HIGHEST


def extended(cells, sides, width):
    for axis, dim in sides:
        count = lax.axis_size(axis)
        ends = count - 1
        head = lax.slice_in_dim(cells, 0, width, axis=dim)
        tail = lax.slice_in_dim(cells, cells.shape[dim] - width, cells.shape[dim], axis=dim)
        cells = jnp.concatenate(
            [
                lax.ppermute(tail, axis, [(i, (i + 1) % count) for i in range(ends)]),
                cells,
                lax.ppermute(head, axis, [((i + 1) % count, i) for i in range(ends)]),
            ],
            axis=dim,
        )
    return cells


def kernel_block(targets, sources):
    spacing = targets[..., 0, :, None] - sources[..., 0, None, :]
    squares = spacing * spacing
    for component in (1, 2):
        spacing = targets[..., component, :, None] - sources[..., component, None, :]
        squares = squares + spacing * spacing
    return jnp.exp(-jnp.sqrt(squares))


def join_children(children):
    pair_count = children.shape[0] // 2
    joined = children.reshape(pair_count, 2, children.shape[1], children.shape[2]).transpose(
        0, 2, 1, 3
    )
    return joined.reshape(pair_count, children.shape[1], 2 * children.shape[2])


def split_children(joined, rank_size):
    parent_count = joined.shape[0]
    halves = joined.reshape(parent_count, joined.shape[1], 2, rank_size).transpose(0, 2, 1, 3)
    return halves.reshape(2 * parent_count, joined.shape[1], rank_size)


def lift_level(children, matrices):
    return jnp.einsum("mkj,mrj->mkr", children, matrices.astype(jnp.float32), precision=highest)


def lower_level(parents, matrices):
    return jnp.einsum("mkr,mrj->mkj", parents, matrices.astype(jnp.float32), precision=highest)


def swap_pairs(values):
    pair_count = values.shape[0] // 2
    return values.reshape((pair_count, 2) + values.shape[1:])[:, ::-1].reshape(values.shape)


def couple_sibling(skeletons, coefficients):
    tile_block = kernel_block(skeletons, swap_pairs(skeletons))
    return jnp.einsum("mij,mkj->mki", tile_block, swap_pairs(coefficients), precision=highest)


def body(
    vectors, points, leaf_basis, near_list, far_list, transfer, skeleton, transfer_top, skeleton_top
):
    rhs_count, cell_count = vectors.shape
    leaf_dev, rank_size, leaf_size = leaf_basis.shape
    slot_count = near_list.shape[1]
    far_slots = far_list.shape[1]
    local_levels = leaf_dev.bit_length() - 1
    devices = lax.axis_size("dev")
    top_levels = devices.bit_length() - 1
    device_id = lax.axis_index("dev")
    reach_leaves = leaf_dev // 2
    wide_leaves = leaf_dev + 2 * reach_leaves
    vector_halo = extended(vectors, (("dev", 1),), reach_leaves * leaf_size)
    point_halo = extended(points, (("dev", 1),), reach_leaves * leaf_size)
    wide_vectors = vector_halo.reshape(rhs_count, wide_leaves, leaf_size)
    wide_points = point_halo.reshape(3, wide_leaves, leaf_size)
    block_leaves = min(4, leaf_dev)

    def near_block(block_index):
        first_leaf = block_index * block_leaves
        offsets = lax.dynamic_slice_in_dim(near_list, first_leaf, block_leaves, 0)
        usable = (jnp.arange(slot_count)[None, :] == 0) | (offsets != 0)
        partners = first_leaf + reach_leaves + jnp.arange(block_leaves)[:, None] + offsets
        own_points = lax.dynamic_slice_in_dim(
            wide_points, first_leaf + reach_leaves, block_leaves, 1
        )
        own_points = jnp.moveaxis(own_points, 0, 1)[:, None]
        partner_points = jnp.moveaxis(wide_points[:, partners], 0, 2)
        tile_block = jnp.where(
            usable[:, :, None, None], kernel_block(own_points, partner_points), 0.0
        ).astype(jnp.bfloat16)
        return jnp.einsum(
            "bsij,kbsj->kbi",
            tile_block,
            wide_vectors[:, partners],
            preferred_element_type=jnp.float32,
        )

    near_blocks = lax.map(near_block, jnp.arange(leaf_dev // block_leaves))
    near_part = jnp.moveaxis(near_blocks, 0, 1).reshape(rhs_count, leaf_dev, leaf_size)
    own_vectors = vectors.reshape(rhs_count, leaf_dev, leaf_size)
    coefficients = [
        jnp.einsum("kti,tri->tkr", own_vectors, leaf_basis, preferred_element_type=jnp.float32)
    ]
    transfers = [None]
    skeletons = [None]
    far_lists = [None]
    for level_index in range(1, local_levels + 1):
        first_row = leaf_dev - (leaf_dev >> level_index - 1)
        level_count = leaf_dev >> level_index
        transfers.append(transfer[first_row : first_row + level_count])
        skeletons.append(
            skeleton[first_row : first_row + level_count].reshape(level_count, 3, rank_size)
        )
        if level_index < local_levels:
            far_lists.append(far_list[first_row : first_row + level_count])
    for level_index in range(1, local_levels + 1):
        coefficients.append(lift_level(join_children(coefficients[-1]), transfers[level_index]))
    middle = leaf_dev - 2
    coef_width = rhs_count * rank_size
    inner_coefs = jnp.concatenate(
        [entry.reshape(entry.shape[0], coef_width) for entry in coefficients[1:local_levels]],
        axis=0,
    )
    cluster_table = jnp.concatenate([inner_coefs, skeleton[:middle]], axis=1)
    cluster_halo = extended(cluster_table, (("dev", 0),), middle)
    root_coef = coefficients[local_levels][0]
    root_skel = skeleton[leaf_dev - 2]
    every_coef, every_skel = (
        lax.all_gather(root_coef.reshape(1, coef_width), "dev", axis=0, tiled=True),
        lax.all_gather(root_skel[None], "dev", axis=0, tiled=True),
    )
    top_coefs = [every_coef.reshape(devices, rhs_count, rank_size)]
    top_skels = [every_skel.reshape(devices, 3, rank_size)]
    top_transfers = [None]
    for step_index in range(1, top_levels + 1):
        first_row = devices - (devices >> step_index - 1)
        level_count = devices >> step_index
        top_transfers.append(transfer_top[first_row : first_row + level_count])
        if step_index < top_levels:
            top_skels.append(
                skeleton_top[first_row : first_row + level_count].reshape(level_count, 3, rank_size)
            )
            top_coefs.append(lift_level(join_children(top_coefs[-1]), top_transfers[step_index]))
    downward = jnp.zeros((1, rhs_count, rank_size), jnp.float32)
    for step_index in range(top_levels - 1, -1, -1):
        downward = split_children(lower_level(downward, top_transfers[step_index + 1]), rank_size)
        downward = downward + couple_sibling(top_skels[step_index], top_coefs[step_index])
    root_field = lax.dynamic_slice_in_dim(downward, device_id, 1, 0)
    downward = root_field
    for level_index in range(local_levels - 1, -1, -1):
        downward = split_children(lower_level(downward, transfers[level_index + 1]), rank_size)
        if level_index >= 1:
            level_count = leaf_dev >> level_index
            first_row = leaf_dev - (leaf_dev >> level_index - 1)
            offsets = far_lists[level_index]
            spot_index = jnp.arange(level_count)[:, None] + offsets
            part_index = spot_index // level_count
            rim_index = (
                (part_index + 1) * middle + first_row + spot_index - part_index * level_count
            )
            partner_rows = cluster_halo[rim_index]
            partner_coef = partner_rows[..., :coef_width].reshape(
                level_count, far_slots, rhs_count, rank_size
            )
            partner_skel = partner_rows[..., coef_width:].reshape(
                level_count, far_slots, 3, rank_size
            )
            tile_block = kernel_block(skeletons[level_index][:, None], partner_skel)
            tile_block = jnp.where((offsets != 0)[:, :, None, None], tile_block, 0.0)
            downward = downward + jnp.einsum(
                "mfij,mfkj->mki", tile_block, partner_coef, precision=highest
            )
    far_part = jnp.einsum(
        "tkr,tri->kti", downward, leaf_basis.astype(jnp.float32), precision=highest
    )
    return (near_part + far_part).reshape(rhs_count, cell_count)


def solution(mesh):
    return jax.shard_map(
        body,
        mesh=mesh,
        in_specs=(
            P(None, "dev"),
            P(None, "dev"),
            P("dev", None, None),
            P("dev", None),
            P("dev", None),
            P("dev", None, None),
            P("dev", None),
            P(),
            P(),
        ),
        out_specs=P(None, "dev"),
        check_vma=False,
    )
```

profile of v0, /device:TPU:1, one launch (start us, length us, event | category | flops | bytes accessed | tf_op | source)
XLA Modules:
  0.0 362.4 jit_solution(9748645149462664096)
XLA Ops:
  20.2 4.5 %collective-permute-start.4 = (f32[62,704]{1,0:T(8,128)}, f32[62,704]{1,0:T(8,128)}, u32[]{:S(2)}, u32[]{:S(2)}) collective-permute-start(f32[62,704]{1,0:T(8,128)} %pad_maximum_fusion.4), channel_id=1, source_target_pairs={{0,1},{1,2},{2,3},{3,4},{4,5},{5,6},{6,7},{7,8},{8,9},{9,10},{10,1... | collective-permute-start | bytes 523784 | tf_op jit(solution)/shard_map/ppermute | solution.py:17
  31.0 3.6 %collective-permute-start.2 = (f32[3,8192]{1,0:T(4,128)}, f32[3,8192]{1,0:T(4,128)}, u32[]{:S(2)}, u32[]{:S(2)}) collective-permute-start(f32[3,8192]{1,0:T(4,128)} %get-tuple-element.126), channel_id=1, source_target_pairs={{0,1},{1,2},{2,3},{3,4},{4,5},{5,6},{6,7},{7,8},{8,9},{9,10},{10,1... | collective-permute-start | bytes 294920 | tf_op jit(solution)/shard_map/ppermute | solution.py:17
  36.0 43.7 %all-gather.1 = f32[32,1,192]{2,1,0:T(1,128)} all-gather(f32[1,1,192]{2,1,0:T(1,128)S(1)} %slice_bitcast_fusion.2), channel_id=1, replica_groups=mesh['dev'=32] {'dev'}, dimensions={0}, use_global_device_ids=true | all-gather | bytes 25344 | tf_op jit(solution)/shard_map/all_gather | solution.py:138
  83.0 36.9 %all-gather = f32[32,1,512]{2,1,0:T(1,128)S(1)} all-gather(f32[1,1,512]{2,1,0:T(1,128)S(1)} %reshape.429), channel_id=1, replica_groups=mesh['dev'=32] {'dev'}, dimensions={0}, use_global_device_ids=true | all-gather | bytes 67584 | tf_op jit(solution)/shard_map/all_gather | solution.py:137
  165.1 3.6 collective-permute-start
  171.4 156.4 %while.12 = (s32[]{:T(128)}, f32[16,8,4,256]{3,1,2,0:T(8,128)}, s32[16]{0:T(128)S(1)}, s32[64,8]{1,0:T(8,128)S(1)}, bf16[8,128,256]{2,0,1:T(8,128)(2,1)S(1)}, /*...) while((s32[]{:T(128)}, f32[16,8,4,256]{3,1,2,0:T(8,128)}, ...), condition=%wide.region_1.2_spmd, body=%wide.region_0.1_spmd.sunk | while | flops 56624340 | bytes 1222617 | solution.py:106
  175.0 6.2 %fusion.346 = f32[16,8,4,256]{3,1,2,0:T(8,128)} fusion(f32[16,8,4,256]{3,1,2,0:T(8,128)} %get-tuple-element.275, s32[]{:T(128)S(6)} %copy.146, bf16[8,4,8,256]{3,0,2,1:T(8,128)(2,1)S(1)} %bitcast.272, f32[4,8,256]{2,1,0:T(8,128)S(1)} %get-tuple-element.254, f32[4,256]{1,0:T(4,128)S(1)} %get-tuple-element.257, ...), kind=kOutput, calls=%fused_computation.11.clone.1 | convolution fusion | flops 56623104 | bytes 274468 | tf_op jit(solution)/shard_map/while/body/eval_jaxpr/bsij,kbsj->kbi/dot_general | solution.py:99
  184.8 6.2 %fusion.346 = f32[16,8,4,256]{3,1,2,0:T(8,128)} fusion(f32[16,8,4,256]{3,1,2,0:T(8,128)} %get-tuple-element.275, s32[]{:T(128)S(6)} %copy.146, bf16[8,4,8,256]{3,0,2,1:T(8,128)(2,1)S(1)} %bitcast.272, f32[4,8,256]{2,1,0:T(8,128)S(1)} %get-tuple-element.254, f32[4,256]{1,0:T(4,128)S(1)} %get-tuple-element.257, ...), kind=kOutput, calls=%fused_computation.11.clone.1 | convolution fusion | flops 56623104 | bytes 274468 | tf_op jit(solution)/shard_map/while/body/eval_jaxpr/bsij,kbsj->kbi/dot_general | solution.py:99
  194.6 6.2 %fusion.346 = f32[16,8,4,256]{3,1,2,0:T(8,128)} fusion(f32[16,8,4,256]{3,1,2,0:T(8,128)} %get-tuple-element.275, s32[]{:T(128)S(6)} %copy.146, bf16[8,4,8,256]{3,0,2,1:T(8,128)(2,1)S(1)} %bitcast.272, f32[4,8,256]{2,1,0:T(8,128)S(1)} %get-tuple-element.254, f32[4,256]{1,0:T(4,128)S(1)} %get-tuple-element.257, ...), kind=kOutput, calls=%fused_computation.11.clone.1 | convolution fusion | flops 56623104 | bytes 274468 | tf_op jit(solution)/shard_map/while/body/eval_jaxpr/bsij,kbsj->kbi/dot_general | solution.py:99
  204.4 6.2 %fusion.346 = f32[16,8,4,256]{3,1,2,0:T(8,128)} fusion(f32[16,8,4,256]{3,1,2,0:T(8,128)} %get-tuple-element.275, s32[]{:T(128)S(6)} %copy.146, bf16[8,4,8,256]{3,0,2,1:T(8,128)(2,1)S(1)} %bitcast.272, f32[4,8,256]{2,1,0:T(8,128)S(1)} %get-tuple-element.254, f32[4,256]{1,0:T(4,128)S(1)} %get-tuple-element.257, ...), kind=kOutput, calls=%fused_computation.11.clone.1 | convolution fusion | flops 56623104 | bytes 274468 | tf_op jit(solution)/shard_map/while/body/eval_jaxpr/bsij,kbsj->kbi/dot_general | solution.py:99
  214.1 6.2 %fusion.346 = f32[16,8,4,256]{3,1,2,0:T(8,128)} fusion(f32[16,8,4,256]{3,1,2,0:T(8,128)} %get-tuple-element.275, s32[]{:T(128)S(6)} %copy.146, bf16[8,4,8,256]{3,0,2,1:T(8,128)(2,1)S(1)} %bitcast.272, f32[4,8,256]{2,1,0:T(8,128)S(1)} %get-tuple-element.254, f32[4,256]{1,0:T(4,128)S(1)} %get-tuple-element.257, ...), kind=kOutput, calls=%fused_computation.11.clone.1 | convolution fusion | flops 56623104 | bytes 274468 | tf_op jit(solution)/shard_map/while/body/eval_jaxpr/bsij,kbsj->kbi/dot_general | solution.py:99
  223.9 6.2 %fusion.346 = f32[16,8,4,256]{3,1,2,0:T(8,128)} fusion(f32[16,8,4,256]{3,1,2,0:T(8,128)} %get-tuple-element.275, s32[]{:T(128)S(6)} %copy.146, bf16[8,4,8,256]{3,0,2,1:T(8,128)(2,1)S(1)} %bitcast.272, f32[4,8,256]{2,1,0:T(8,128)S(1)} %get-tuple-element.254, f32[4,256]{1,0:T(4,128)S(1)} %get-tuple-element.257, ...), kind=kOutput, calls=%fused_computation.11.clone.1 | convolution fusion | flops 56623104 | bytes 274468 | tf_op jit(solution)/shard_map/while/body/eval_jaxpr/bsij,kbsj->kbi/dot_general | solution.py:99
  233.7 6.2 %fusion.346 = f32[16,8,4,256]{3,1,2,0:T(8,128)} fusion(f32[16,8,4,256]{3,1,2,0:T(8,128)} %get-tuple-element.275, s32[]{:T(128)S(6)} %copy.146, bf16[8,4,8,256]{3,0,2,1:T(8,128)(2,1)S(1)} %bitcast.272, f32[4,8,256]{2,1,0:T(8,128)S(1)} %get-tuple-element.254, f32[4,256]{1,0:T(4,128)S(1)} %get-tuple-element.257, ...), kind=kOutput, calls=%fused_computation.11.clone.1 | convolution fusion | flops 56623104 | bytes 274468 | tf_op jit(solution)/shard_map/while/body/eval_jaxpr/bsij,kbsj->kbi/dot_general | solution.py:99
  243.5 6.2 %fusion.346 = f32[16,8,4,256]{3,1,2,0:T(8,128)} fusion(f32[16,8,4,256]{3,1,2,0:T(8,128)} %get-tuple-element.275, s32[]{:T(128)S(6)} %copy.146, bf16[8,4,8,256]{3,0,2,1:T(8,128)(2,1)S(1)} %bitcast.272, f32[4,8,256]{2,1,0:T(8,128)S(1)} %get-tuple-element.254, f32[4,256]{1,0:T(4,128)S(1)} %get-tuple-element.257, ...), kind=kOutput, calls=%fused_computation.11.clone.1 | convolution fusion | flops 56623104 | bytes 274468 | tf_op jit(solution)/shard_map/while/body/eval_jaxpr/bsij,kbsj->kbi/dot_general | solution.py:99
  253.2 6.2 %fusion.346 = f32[16,8,4,256]{3,1,2,0:T(8,128)} fusion(f32[16,8,4,256]{3,1,2,0:T(8,128)} %get-tuple-element.275, s32[]{:T(128)S(6)} %copy.146, bf16[8,4,8,256]{3,0,2,1:T(8,128)(2,1)S(1)} %bitcast.272, f32[4,8,256]{2,1,0:T(8,128)S(1)} %get-tuple-element.254, f32[4,256]{1,0:T(4,128)S(1)} %get-tuple-element.257, ...), kind=kOutput, calls=%fused_computation.11.clone.1 | convolution fusion | flops 56623104 | bytes 274468 | tf_op jit(solution)/shard_map/while/body/eval_jaxpr/bsij,kbsj->kbi/dot_general | solution.py:99
  263.0 6.2 %fusion.346 = f32[16,8,4,256]{3,1,2,0:T(8,128)} fusion(f32[16,8,4,256]{3,1,2,0:T(8,128)} %get-tuple-element.275, s32[]{:T(128)S(6)} %copy.146, bf16[8,4,8,256]{3,0,2,1:T(8,128)(2,1)S(1)} %bitcast.272, f32[4,8,256]{2,1,0:T(8,128)S(1)} %get-tuple-element.254, f32[4,256]{1,0:T(4,128)S(1)} %get-tuple-element.257, ...), kind=kOutput, calls=%fused_computation.11.clone.1 | convolution fusion | flops 56623104 | bytes 274468 | tf_op jit(solution)/shard_map/while/body/eval_jaxpr/bsij,kbsj->kbi/dot_general | solution.py:99
  272.8 6.2 %fusion.346 = f32[16,8,4,256]{3,1,2,0:T(8,128)} fusion(f32[16,8,4,256]{3,1,2,0:T(8,128)} %get-tuple-element.275, s32[]{:T(128)S(6)} %copy.146, bf16[8,4,8,256]{3,0,2,1:T(8,128)(2,1)S(1)} %bitcast.272, f32[4,8,256]{2,1,0:T(8,128)S(1)} %get-tuple-element.254, f32[4,256]{1,0:T(4,128)S(1)} %get-tuple-element.257, ...), kind=kOutput, calls=%fused_computation.11.clone.1 | convolution fusion | flops 56623104 | bytes 274468 | tf_op jit(solution)/shard_map/while/body/eval_jaxpr/bsij,kbsj->kbi/dot_general | solution.py:99
  282.5 6.2 %fusion.346 = f32[16,8,4,256]{3,1,2,0:T(8,128)} fusion(f32[16,8,4,256]{3,1,2,0:T(8,128)} %get-tuple-element.275, s32[]{:T(128)S(6)} %copy.146, bf16[8,4,8,256]{3,0,2,1:T(8,128)(2,1)S(1)} %bitcast.272, f32[4,8,256]{2,1,0:T(8,128)S(1)} %get-tuple-element.254, f32[4,256]{1,0:T(4,128)S(1)} %get-tuple-element.257, ...), kind=kOutput, calls=%fused_computation.11.clone.1 | convolution fusion | flops 56623104 | bytes 274468 | tf_op jit(solution)/shard_map/while/body/eval_jaxpr/bsij,kbsj->kbi/dot_general | solution.py:99
  292.3 6.2 %fusion.346 = f32[16,8,4,256]{3,1,2,0:T(8,128)} fusion(f32[16,8,4,256]{3,1,2,0:T(8,128)} %get-tuple-element.275, s32[]{:T(128)S(6)} %copy.146, bf16[8,4,8,256]{3,0,2,1:T(8,128)(2,1)S(1)} %bitcast.272, f32[4,8,256]{2,1,0:T(8,128)S(1)} %get-tuple-element.254, f32[4,256]{1,0:T(4,128)S(1)} %get-tuple-element.257, ...), kind=kOutput, calls=%fused_computation.11.clone.1 | convolution fusion | flops 56623104 | bytes 274468 | tf_op jit(solution)/shard_map/while/body/eval_jaxpr/bsij,kbsj->kbi/dot_general | solution.py:99
  302.1 6.2 %fusion.346 = f32[16,8,4,256]{3,1,2,0:T(8,128)} fusion(f32[16,8,4,256]{3,1,2,0:T(8,128)} %get-tuple-element.275, s32[]{:T(128)S(6)} %copy.146, bf16[8,4,8,256]{3,0,2,1:T(8,128)(2,1)S(1)} %bitcast.272, f32[4,8,256]{2,1,0:T(8,128)S(1)} %get-tuple-element.254, f32[4,256]{1,0:T(4,128)S(1)} %get-tuple-element.257, ...), kind=kOutput, calls=%fused_computation.11.clone.1 | convolution fusion | flops 56623104 | bytes 274468 | tf_op jit(solution)/shard_map/while/body/eval_jaxpr/bsij,kbsj->kbi/dot_general | solution.py:99
  311.9 6.2 %fusion.346 = f32[16,8,4,256]{3,1,2,0:T(8,128)} fusion(f32[16,8,4,256]{3,1,2,0:T(8,128)} %get-tuple-element.275, s32[]{:T(128)S(6)} %copy.146, bf16[8,4,8,256]{3,0,2,1:T(8,128)(2,1)S(1)} %bitcast.272, f32[4,8,256]{2,1,0:T(8,128)S(1)} %get-tuple-element.254, f32[4,256]{1,0:T(4,128)S(1)} %get-tuple-element.257, ...), kind=kOutput, calls=%fused_computation.11.clone.1 | convolution fusion | flops 56623104 | bytes 274468 | tf_op jit(solution)/shard_map/while/body/eval_jaxpr/bsij,kbsj->kbi/dot_general | solution.py:99
  321.6 6.2 %fusion.346 = f32[16,8,4,256]{3,1,2,0:T(8,128)} fusion(f32[16,8,4,256]{3,1,2,0:T(8,128)} %get-tuple-element.275, s32[]{:T(128)S(6)} %copy.146, bf16[8,4,8,256]{3,0,2,1:T(8,128)(2,1)S(1)} %bitcast.272, f32[4,8,256]{2,1,0:T(8,128)S(1)} %get-tuple-element.254, f32[4,256]{1,0:T(4,128)S(1)} %get-tuple-element.257, ...), kind=kOutput, calls=%fused_computation.11.clone.1 | convolution fusion | flops 56623104 | bytes 274468 | tf_op jit(solution)/shard_map/while/body/eval_jaxpr/bsij,kbsj->kbi/dot_general | solution.py:99
  342.8 4.2 %fusion.49 = f32[16,8,64]{2,1,0:T(8,128)S(1)} fusion(f32[16,8,64]{2,1,0:T(8,128)S(1)} %bitcast.310, f32[16,4,8,64]{3,2,1,0:T(8,128)} %reshape.352, f32[16,4,64]{2,1,0:T(4,128)S(1)} %copy.102, f32[16,64]{1,0:T(8,128)S(1)} %bitcast.333, f32[16,4,64]{2,1,0:T(4,128)S(1)} %copy.101, f32[16,64]{1,0:T(8,128)S(1)} %bitcast.334, f32[16,4,64]{2,1,0:T(4,128)S(1)} %copy.100, ...), kind=kOutput, calls=%fused_computation.65 | convolution fusion | flops 27795456 | bytes 258112 | tf_op jit(solution)/shard_map/mfij,mfkj->mki/dot_general | solution.py:178
  352.1 7.5 %fusion.43 = f32[32,8,64]{2,1,0:T(8,128)S(1)} fusion(f32[32,8,64]{2,1,0:T(8,128)S(1)} %bitcast.301, f32[32,4,8,64]{3,2,1,0:T(8,128)} %reshape.355, f32[32,4,64]{2,1,0:T(4,128)S(1)} %copy.108, f32[32,64]{1,0:T(8,128)S(1)} %bitcast.324, f32[32,4,64]{2,1,0:T(4,128)S(1)} %copy.107, f32[32,64]{1,0:T(8,128)} %bitcast.325, f32[32,4,64]{2,1,0:T(4,128)S(1)} %copy.106, ...), kind=kOutput, calls=%fused_computation.62 | convolution fusion | flops 55590912 | bytes 516224 | tf_op jit(solution)/shard_map/mfij,mfkj->mki/dot_general | solution.py:178
  (696 shorter events, 146.4 us)
Async XLA Ops:
  3.2 21.5 %copy-start.3 = (bf16[8,16384]{1,0:T(8,128)(2,1)S(1)}, bf16[8,16384]{1,0:T(8,128)(2,1)}, u32[]{:S(2)}) copy-start(bf16[8,16384]{1,0:T(8,128)(2,1)} %param.11) | copy-start | bytes 786436
  16.6 112.4 %copy-start.5 = (f32[62,512]{1,0:T(8,128)}, f32[62,512]{1,0:T(8,128)S(1)}, u32[]{:S(2)}) copy-start(f32[62,512]{1,0:T(8,128)S(1)} %concatenate.48) | copy-start | bytes 380932
  18.3 309.6 %collective-permute-start.5 = (f32[62,704]{1,0:T(8,128)}, f32[62,704]{1,0:T(8,128)}, u32[]{:S(2)}, u32[]{:S(2)}) collective-permute-start(f32[62,704]{1,0:T(8,128)} %pad_maximum_fusion.4), channel_id=1, source_target_pairs={{1,0},{2,1},{3,2},{4,3},{5,4},{6,5},{7,6},{8,7},{9,8},{10,9},{11,1... | collective-permute-start | bytes 523784 | tf_op jit(solution)/shard_map/ppermute | solution.py:19
  20.2 307.6 %collective-permute-start.4 = (f32[62,704]{1,0:T(8,128)}, f32[62,704]{1,0:T(8,128)}, u32[]{:S(2)}, u32[]{:S(2)}) collective-permute-start(f32[62,704]{1,0:T(8,128)} %pad_maximum_fusion.4), channel_id=1, source_target_pairs={{0,1},{1,2},{2,3},{3,4},{4,5},{5,6},{6,7},{7,8},{8,9},{9,10},{10,1... | collective-permute-start | bytes 523784 | tf_op jit(solution)/shard_map/ppermute | solution.py:17
  25.5 144.4 %collective-permute-start.1 = (bf16[8,8192]{1,0:T(8,128)(2,1)}, bf16[8,8192]{1,0:T(8,128)(2,1)}, u32[]{:S(2)}, u32[]{:S(2)}) collective-permute-start(bf16[8,8192]{1,0:T(8,128)(2,1)} %get-tuple-element.129), channel_id=1, source_target_pairs={{1,0},{2,1},{3,2},{4,3},{5,4},{6,5},{7,6},{8,7},{9,8},{10,9},{11,1... | collective-permute-start | bytes 393224 | tf_op jit(solution)/shard_map/ppermute | solution.py:19
  29.1 136.0 %collective-permute-start.3 = (f32[3,8192]{1,0:T(4,128)}, f32[3,8192]{1,0:T(4,128)}, u32[]{:S(2)}, u32[]{:S(2)}) collective-permute-start(f32[3,8192]{1,0:T(4,128)} %get-tuple-element.127), channel_id=1, source_target_pairs={{1,0},{2,1},{3,2},{4,3},{5,4},{6,5},{7,6},{8,7},{9,8},{10,9},{11,1... | collective-permute-start | bytes 294920 | tf_op jit(solution)/shard_map/ppermute | solution.py:19
  31.0 137.7 %collective-permute-start.2 = (f32[3,8192]{1,0:T(4,128)}, f32[3,8192]{1,0:T(4,128)}, u32[]{:S(2)}, u32[]{:S(2)}) collective-permute-start(f32[3,8192]{1,0:T(4,128)} %get-tuple-element.126), channel_id=1, source_target_pairs={{0,1},{1,2},{2,3},{3,4},{4,5},{5,6},{6,7},{7,8},{8,9},{9,10},{10,1... | collective-permute-start | bytes 294920 | tf_op jit(solution)/shard_map/ppermute | solution.py:17
  81.9 47.8 %copy-start.12 = (s32[62,4]{0,1:T(4,128)S(1)}, s32[62,4]{0,1:T(4,128)}, u32[]{:S(2)}) copy-start(s32[62,4]{0,1:T(4,128)} %param.15) | copy-start | bytes 2980
  82.8 44.5 %copy-start.4 = (bf16[31,64,128]{2,1,0:T(8,128)(2,1)S(1)}, bf16[31,64,128]{2,1,0:T(8,128)(2,1)}, u32[]{:S(2)}) copy-start(bf16[31,64,128]{2,1,0:T(8,128)(2,1)} %param.18) | copy-start | bytes 1523716
  82.8 45.3 %copy-start.20 = (f32[30,192]{1,0:T(8,128)S(1)}, f32[30,192]{1,0:T(8,128)}, u32[]{:S(2)}) copy-start(f32[30,192]{1,0:T(8,128)} %param.19) | copy-start | bytes 69124
  82.8 46.4 %copy-start.8 = (f32[63,192]{1,0:T(8,128)S(1)}, f32[63,192]{1,0:T(8,128)}, u32[]{:S(2)}) copy-start(f32[63,192]{1,0:T(8,128)} %param.17) | copy-start | bytes 145156
  82.9 54.8 %copy-start.11 = (f32[16,2,3,64]{3,2,1,0:T(4,128)S(1)}, f32[16,2,3,64]{3,2,1,0:T(4,128)}, u32[]{:S(2)}) copy-start(f32[16,2,3,64]{3,2,1,0:T(4,128)} %reshape_reshape.24) | copy-start | bytes 73732
  82.9 55.5 %copy-start.13 = (f32[32,3,64]{2,1,0:T(4,128)S(1)}, f32[32,3,64]{2,1,0:T(4,128)}, u32[]{:S(2)}) copy-start(f32[32,3,64]{2,1,0:T(4,128)} %reshape.334) | copy-start | bytes 73732
  144.4 8.6 %copy-start.24 = (s32[8,4]{0,1:T(4,128)S(1)}, s32[8,4]{0,1:T(4,128)}, u32[]{:S(2)}) copy-start(s32[8,4]{0,1:T(4,128)} %compare_select_fusion.3) | copy-start | bytes 388
  144.7 16.2 %copy-start.14 = (f32[16,2,8,64]{3,2,1,0:T(8,128)S(1)}, f32[16,2,8,64]{3,2,1,0:T(8,128)}, u32[]{:S(2)}) copy-start(f32[16,2,8,64]{3,2,1,0:T(8,128)} %rev.35) | copy-start | bytes 196612
  147.5 17.6 %copy-start.15 = (bf16[8,8192]{1,0:T(8,128)(2,1)S(1)}, bf16[8,8192]{1,0:T(8,128)(2,1)}, u32[]{:S(2)}) copy-start(bf16[8,8192]{1,0:T(8,128)(2,1)} %get-tuple-element.128) | copy-start | bytes 393220
  147.5 21.2 %copy-start.6 = (f32[3,16384]{1,0:T(4,128)S(1)}, f32[3,16384]{1,0:T(4,128)}, u32[]{:S(2)}) copy-start(f32[3,16384]{1,0:T(4,128)} %param.12) | copy-start | bytes 589828
  165.1 5.3 %collective-permute-start = (bf16[8,8192]{1,0:T(8,128)(2,1)S(1)}, bf16[8,8192]{1,0:T(8,128)(2,1)S(1)}, u32[]{:S(2)}, u32[]{:S(2)}) collective-permute-start(bf16[8,8192]{1,0:T(8,128)(2,1)S(1)} %copy-done.15), channel_id=1, source_target_pairs={{0,1},{1,2},{2,3},{3,4},{4,5},{5,6},{6,7},{7,8},{8,9},{9,10},{10,1... | collective-permute-start | bytes 393224 | tf_op jit(solution)/shard_map/ppermute | solution.py:17
  194.6 6.2 %copy-start.39 = (s32[16]{0:T(128)S(1)}, s32[16]{0:T(128)}, u32[]{:S(2)}) copy-start(s32[16]{0:T(128)} %copy-done.38) | copy-start | bytes 196 | tf_op jit(solution)/shard_map/while
  204.4 6.2 %copy-start.39 = (s32[16]{0:T(128)S(1)}, s32[16]{0:T(128)}, u32[]{:S(2)}) copy-start(s32[16]{0:T(128)} %copy-done.38) | copy-start | bytes 196 | tf_op jit(solution)/shard_map/while
  214.1 6.2 %copy-start.39 = (s32[16]{0:T(128)S(1)}, s32[16]{0:T(128)}, u32[]{:S(2)}) copy-start(s32[16]{0:T(128)} %copy-done.38) | copy-start | bytes 196 | tf_op jit(solution)/shard_map/while
  223.9 6.2 %copy-start.39 = (s32[16]{0:T(128)S(1)}, s32[16]{0:T(128)}, u32[]{:S(2)}) copy-start(s32[16]{0:T(128)} %copy-done.38) | copy-start | bytes 196 | tf_op jit(solution)/shard_map/while
  233.7 6.2 %copy-start.39 = (s32[16]{0:T(128)S(1)}, s32[16]{0:T(128)}, u32[]{:S(2)}) copy-start(s32[16]{0:T(128)} %copy-done.38) | copy-start | bytes 196 | tf_op jit(solution)/shard_map/while
  342.8 6.3 %slice-start.1 = ((f32[32,4,704]{2,1,0:T(4,128)}), f32[32,4,192]{2,1,0:T(4,128)S(1)}, s32[]{:S(2)}) async-start(f32[32,4,704]{2,1,0:T(4,128)} %reshape.408), calls=%async_computation.1 | async-start | bytes 262144 | tf_op jit(solution)/shard_map/slice | solution.py:173
  (92 other events, 332.4 us)
where the time goes:
time: 365 us; the launch traced here: 362 us
  matrix products  134 us (37%)
  local copies, waits for them, and re-layouts  89.9 us (25%)
  blocking collectives  80.6 us (22%)
  other arithmetic  26.9 us (7%)
  starting transfers between devices  17.5 us (5%)
  loops' own time  12 us (3%)
    dot_general x16, matrix products, near_block(): jnp.einsum('bsij,kbsj->kbi', tile_block, wide_vectors[:, partners], prefe...  98.8 us
    all_gather x1, blocking collectives, body(): lax.all_gather(root_skel[None], 'dev', axis=0, tiled=True)  43.7 us
    all_gather x1, blocking collectives, body(): lax.all_gather(root_coef.reshape(1, coef_width), 'dev', axis=0, tiled=True)  36.9 us
    dot_general x5, matrix products, body(): jnp.einsum('mfij,mfkj->mki', tile_block, partner_coef, precision=highest)  15.5 us
    another operation x1, loops' own time, body(): near_blocks = lax.map(near_block, jnp.arange(leaf_dev // block_leaves))  12 us
    ppermute x3, starting transfers between devices, extended(): lax.ppermute(tail, axis, [(i, (i + 1) % count) for i in range(ends)])  11.7 us
    or x16, other arithmetic, near_block(): usable = (jnp.arange(slot_count)[None, :] == 0) | (offsets != 0)  11.1 us
    dynamic_slice x16, local copies, waits for them, and re-layouts, body(): near_blocks = lax.map(near_block, jnp.arange(leaf_dev // block_leaves))  10.4 us
  transfers between devices with their start and end apart: 6, of which 1 were waited for; matrix products, arithmetic and copies ran while one was open for 55% of the time, Pallas kernels for 0%

commit v1 on v0

v1 whole, which is shorter than its diff:
```python
import functools
import math

import jax
import jax.numpy as jnp
from jax import lax
from jax.experimental import pallas as pl
from jax.experimental.pallas import tpu as pltpu
from jax.sharding import PartitionSpec as P

F32 = jnp.float32
BF16 = jnp.bfloat16
LOG2E = math.log2(math.e)
TINY = 1e-30
FEATURES = 48
GROUP = 4
VMEM_BYTES = 56 * 1024 * 1024


def neighbours(cells):
    count = lax.axis_size("dev")
    ends = count - 1
    from_left = lax.ppermute(cells, "dev", [(i, i + 1) for i in range(ends)])
    from_right = lax.ppermute(cells, "dev", [(i + 1, i) for i in range(ends)])
    return from_left, from_right


def loop(count, unroll, step):
    unroll = min(unroll, count)

    def several(index, carry):
        for part in range(unroll):
            step(index * unroll + part)
        return carry

    lax.fori_loop(0, count // unroll, several, 0)


def level_row(leaf_count, level):
    return leaf_count - (leaf_count >> (level - 1))


def three_pieces(values):
    first = values.astype(BF16).astype(F32)
    rest = values - first
    second = rest.astype(BF16).astype(F32)
    return first, second, rest - second


def distance_factors(cells):
    scaled = cells * LOG2E
    norms = jnp.sum(scaled * scaled, axis=0, keepdims=True)
    row = lax.broadcasted_iota(jnp.int32, scaled.shape, 0)
    source = jnp.where(row == 3, norms, jnp.where(row == 4, 1.0, scaled))
    target = jnp.where(row == 3, 1.0, jnp.where(row == 4, norms, -2.0 * scaled))
    s1, s2, s3 = three_pieces(source)
    t1, t2, t3 = three_pieces(target)
    sources = jnp.concatenate([s1, s1, s2, s2, s1, s3], axis=0).astype(BF16)
    targets = jnp.concatenate([t1, t2, t1, t2, t3, t1], axis=0).astype(BF16)
    return sources, targets


def decay(squares):
    kept = jnp.maximum(squares, TINY)
    return jnp.exp2(-(kept * lax.rsqrt(kept)))


def product_rows(left, right):
    return lax.dot_general(left, right, (((0,), (0,)), ((), ())), preferred_element_type=F32)


def product(left, right):
    return lax.dot_general(left, right, (((1,), (0,)), ((), ())), preferred_element_type=F32)


def product_across(left, right):
    return lax.dot_general(left, right, (((1,), (1,)), ((), ())), preferred_element_type=F32)


def two_pieces(values):
    first = values.astype(BF16).astype(F32)
    return jnp.concatenate([first, values - first], axis=0).astype(BF16)


def fold(values):
    half = values.shape[0] // 2
    return values[:half] + values[half:]


def skeleton_cells(row):
    rank = row.shape[1] // 3
    parts = [row[:, c * rank : (c + 1) * rank] for c in range(3)]
    return jnp.concatenate(parts + [jnp.zeros((5, rank), F32)], axis=0)


def up_kernel(vec_ref, basis_ref, transfer_ref, skeleton_ref, table_ref, pair_ref):
    leaf_dev, rank, leaf = basis_ref.shape
    local = leaf_dev.bit_length() - 1

    def leaf_pair(pair):
        halves = []
        for part in range(2):
            spot = pair * 2 + part
            own = vec_ref[:, pl.ds(pl.multiple_of(spot * leaf, leaf), leaf)]
            halves.append(product_across(own, basis_ref[spot]))
        pair_ref[pair] = jnp.concatenate(halves, axis=1)

    loop(leaf_dev // 2, 8, leaf_pair)
    joined = [pair_ref[pair] for pair in range(leaf_dev // 2)]
    for level in range(1, local + 1):
        first = level_row(leaf_dev, level)
        coefs = []
        for spot in range(leaf_dev >> level):
            coef = fold(product_across(two_pieces(joined[spot]), transfer_ref[first + spot]))
            cells = skeleton_cells(skeleton_ref[pl.ds(first + spot, 1), :])
            table_ref[first + spot] = jnp.concatenate([coef, cells], axis=1)
            coefs.append(coef)
        joined = [
            jnp.concatenate(coefs[2 * spot : 2 * spot + 2], axis=1)
            for spot in range(len(coefs) // 2)
        ]


def near_kernel(
    list_ref,
    points_ref,
    points_left_ref,
    points_right_ref,
    vec_ref,
    vec_left_ref,
    vec_right_ref,
    out_ref,
    source_ref,
    target_ref,
    wide_vec_ref,
    task_target_ref,
    task_source_ref,
):
    leaf_dev, slots = list_ref.shape
    leaf = points_ref.shape[1] // leaf_dev
    reach = leaf_dev // 2
    wide = leaf_dev + 2 * reach
    chunk = 4 * leaf

    def cells_of(ref, start):
        part = ref[:, pl.ds(start, chunk)]
        return jnp.concatenate([part, jnp.zeros((5, chunk), F32)], axis=0)

    def fill(points, vecs, base, own):
        def step(index):
            start = pl.multiple_of(index * chunk, chunk)
            spot = pl.multiple_of(base + start, chunk)
            sources, targets = distance_factors(cells_of(points, start))
            source_ref[:, pl.ds(spot, chunk)] = sources
            if own:
                target_ref[:, pl.ds(start, chunk)] = targets
                out_ref[:, pl.ds(start, chunk)] = jnp.zeros((out_ref.shape[0], chunk), F32)
            wide_vec_ref[:, pl.ds(spot, chunk)] = vecs[:, pl.ds(start, chunk)].astype(F32)

        loop(points.shape[1] // chunk, 2, step)

    fill(points_left_ref, vec_left_ref, 0, False)
    fill(points_ref, vec_ref, reach * leaf, True)
    fill(points_right_ref, vec_right_ref, (reach + leaf_dev) * leaf, False)
    empty = pl.ds(wide * leaf, leaf)
    source_ref[:, empty] = jnp.zeros((FEATURES, leaf), BF16)
    wide_vec_ref[:, empty] = jnp.zeros((wide_vec_ref.shape[0], leaf), F32)

    def enlist(target, count):
        for slot in range(slots):
            offset = list_ref[target, slot]
            task_target_ref[count] = target
            task_source_ref[count] = target + offset + reach
            if slot == 0:
                count = count + 1
            else:
                count = count + jnp.where(offset != 0, 1, 0)
        return count

    count = lax.fori_loop(0, leaf_dev, enlist, 0)
    for extra in range(GROUP):
        task_target_ref[count + extra] = 0
        task_source_ref[count + extra] = wide

    def several(index, carry):
        results = []
        for part in range(GROUP):
            target = pl.multiple_of(task_target_ref[index * GROUP + part] * leaf, leaf)
            source = pl.multiple_of(task_source_ref[index * GROUP + part] * leaf, leaf)
            squares = product_rows(
                source_ref[:, pl.ds(source, leaf)], target_ref[:, pl.ds(target, leaf)]
            )
            tile = decay(squares).astype(BF16)
            vec = wide_vec_ref[:, pl.ds(source, leaf)].astype(BF16)
            results.append((target, product(vec, tile)))
        for target, result in results:
            out_ref[:, pl.ds(target, leaf)] += result
        return carry

    lax.fori_loop(0, (count + GROUP - 1) // GROUP, several, 0)


def couple(cells, rows, weights):
    rank = cells.shape[1]
    coefs = jnp.concatenate(
        [row[:, :rank] * weight for row, weight in zip(rows, weights)], axis=1
    )
    partner_cells = jnp.concatenate([row[:, rank:] for row in rows], axis=1)
    sources, _ = distance_factors(partner_cells)
    _, targets = distance_factors(cells)
    tile = decay(product_rows(sources, targets))
    main = tile.astype(BF16)
    rest = (tile - main.astype(F32)).astype(BF16)
    pieces = two_pieces(coefs)
    return fold(product(pieces, main) + product(pieces, rest))


def down_kernel(
    far_ref,
    near_ref,
    basis_ref,
    transfer_ref,
    own_ref,
    left_ref,
    right_ref,
    roots_ref,
    transfer_top_ref,
    skeleton_top_ref,
    out_ref,
    wide_ref,
    top_ref,
    coupled_ref,
    field_ref,
):
    leaf_dev, rank, leaf = basis_ref.shape
    devices = roots_ref.shape[0]
    local = leaf_dev.bit_length() - 1
    top = devices.bit_length() - 1
    rows = leaf_dev - 1
    me = lax.axis_index("dev")

    for part, ref in enumerate((left_ref, own_ref, right_ref)):
        wide_ref[part * rows : (part + 1) * rows] = ref[...]
    top_ref[0:devices] = roots_ref[...]

    def top_row(step, spot):
        if step == 0:
            return spot
        return devices + devices - (devices >> (step - 1)) + spot

    for step in range(1, top):
        first = devices - (devices >> (step - 1))

        def lift(spot, step=step, first=first):
            joined = jnp.concatenate(
                [top_ref[top_row(step - 1, 2 * spot + part)][:, :rank] for part in range(2)],
                axis=1,
            )
            coef = fold(product_across(two_pieces(joined), transfer_top_ref[first + spot]))
            cells = skeleton_cells(skeleton_top_ref[pl.ds(first + spot, 1), :])
            top_ref[top_row(step, spot)] = jnp.concatenate([coef, cells], axis=1)

        loop(devices >> step, 16, lift)

    for level in range(1, local):
        first = level_row(leaf_dev, level)
        count = leaf_dev >> level

        def couple_pair(pair, first=first, count=count):
            halves = []
            for part in range(2):
                spot = pair * 2 + part
                partners, weights = [], []
                for slot in range(far_ref.shape[1]):
                    offset = far_ref[first + spot, slot]
                    partner = spot + offset
                    side = jnp.where(partner < 0, 0, jnp.where(partner < count, 1, 2))
                    partners.append(wide_ref[side * rows + first + partner - (side - 1) * count])
                    weights.append(jnp.where(offset != 0, 1.0, 0.0))
                mine = wide_ref[rows + first + spot]
                halves.append(couple(mine[:, rank:], partners, weights))
            coupled_ref[first // 2 + pair] = jnp.concatenate(halves, axis=1)

        loop(count // 2, 2, couple_pair)

    field = None
    for step in range(top - 1, -1, -1):
        spot = me >> step
        mine = top_ref[top_row(step, spot)]
        sibling = top_ref[top_row(step, spot ^ 1)]
        coupled = couple(mine[:, rank:], [sibling], [1.0])
        if field is None:
            field = coupled
        else:
            parent = devices - (devices >> step) + (spot >> 1)
            both = fold(product(two_pieces(field), transfer_top_ref[parent]))
            field = jnp.where((spot & 1) == 1, both[:, rank:], both[:, :rank]) + coupled

    fields = [field]
    for level in range(local - 1, -1, -1):
        first = level_row(leaf_dev, level + 1)
        below = []
        for spot, parent in enumerate(fields):
            both = fold(product(two_pieces(parent), transfer_ref[first + spot]))
            if level >= 1:
                both = both + coupled_ref[level_row(leaf_dev, level) // 2 + spot]
                below += [both[:, :rank], both[:, rank:]]
            else:
                field_ref[spot] = both
        fields = below

    def expand(pair):
        both = field_ref[pair]
        for part in range(2):
            spot = pair * 2 + part
            pieces = two_pieces(both[:, part * rank : (part + 1) * rank])
            columns = pl.ds(pl.multiple_of(spot * leaf, leaf), leaf)
            out_ref[:, columns] = near_ref[:, columns] + fold(product(pieces, basis_ref[spot]))

    loop(leaf_dev // 2, 4, expand)


def body(
    vectors, points, leaf_basis, near_list, far_list, transfer, skeleton, transfer_top, skeleton_top
):
    rhs, cells = vectors.shape
    leaf_dev, rank, leaf = leaf_basis.shape
    slots = near_list.shape[1]
    devices = lax.axis_size("dev")
    reach = leaf_dev // 2
    wide = leaf_dev + 2 * reach
    rows = leaf_dev - 1
    edge = reach * leaf
    vmem = pl.BlockSpec(memory_space=pltpu.VMEM)
    smem = pl.BlockSpec(memory_space=pltpu.SMEM)
    params = pltpu.CompilerParams(vmem_limit_bytes=VMEM_BYTES)

    ends = devices - 1
    to_right = [(i, i + 1) for i in range(ends)]
    to_left = [(i + 1, i) for i in range(ends)]
    points_left = lax.ppermute(points[:, cells - edge :], "dev", to_right)
    points_right = lax.ppermute(points[:, :edge], "dev", to_left)
    vec_left = lax.ppermute(vectors[:, cells - edge :], "dev", to_right)
    vec_right = lax.ppermute(vectors[:, :edge], "dev", to_left)

    table = pl.pallas_call(
        up_kernel,
        out_shape=jax.ShapeDtypeStruct((rows, rhs, 2 * rank), F32),
        in_specs=[vmem] * 4,
        out_specs=vmem,
        scratch_shapes=[pltpu.VMEM((leaf_dev // 2, rhs, 2 * rank), F32)],
        compiler_params=params,
        cost_estimate=pl.CostEstimate(
            flops=2 * 256 * 256 * 256 * 64, bytes_accessed=4 * 2**20, transcendentals=0
        ),
        name="upward",
    )(vectors, leaf_basis, transfer, skeleton)

    table_left = lax.ppermute(table, "dev", to_right)
    table_right = lax.ppermute(table, "dev", to_left)
    roots = lax.all_gather(table[rows - 1 :], "dev", axis=0, tiled=True)

    tasks = leaf_dev * slots + 2 * GROUP
    near = pl.pallas_call(
        near_kernel,
        out_shape=jax.ShapeDtypeStruct((rhs, cells), F32),
        in_specs=[smem] + [vmem] * 6,
        out_specs=vmem,
        scratch_shapes=[
            pltpu.VMEM((FEATURES, (wide + 1) * leaf), BF16),
            pltpu.VMEM((FEATURES, cells), BF16),
            pltpu.VMEM((rhs, (wide + 1) * leaf), F32),
            pltpu.SMEM((tasks,), jnp.int32),
            pltpu.SMEM((tasks,), jnp.int32),
        ],
        compiler_params=params,
        cost_estimate=pl.CostEstimate(
            flops=2 * 256 * 256 * 256 * 64 * 20, bytes_accessed=2 * 2**20, transcendentals=2**25
        ),
        name="near",
    )(near_list, points, points_left, points_right, vectors, vec_left, vec_right)

    return pl.pallas_call(
        down_kernel,
        out_shape=jax.ShapeDtypeStruct((rhs, cells), F32),
        in_specs=[smem] + [vmem] * 9,
        out_specs=vmem,
        scratch_shapes=[
            pltpu.VMEM((3 * rows, rhs, 2 * rank), F32),
            pltpu.VMEM((2 * devices, rhs, 2 * rank), F32),
            pltpu.VMEM((leaf_dev // 2, rhs, 2 * rank), F32),
            pltpu.VMEM((leaf_dev // 2, rhs, 2 * rank), F32),
        ],
        compiler_params=params,
        cost_estimate=pl.CostEstimate(
            flops=2 * 256 * 256 * 256 * 64, bytes_accessed=4 * 2**20, transcendentals=2**21
        ),
        name="downward",
    )(
        far_list,
        near,
        leaf_basis,
        transfer,
        table,
        table_left,
        table_right,
        roots,
        transfer_top,
        skeleton_top,
    )


def solution(mesh):
    return jax.shard_map(
        body,
        mesh=mesh,
        in_specs=(
            P(None, "dev"),
            P(None, "dev"),
            P("dev", None, None),
            P("dev", None),
            P("dev", None),
            P("dev", None, None),
            P("dev", None),
            P(),
            P(),
        ),
        out_specs=P(None, "dev"),
        check_vma=False,
    )
```

time: 365 us -> 175 us (0.48)
  the two profiles are of different devices: /device:TPU:1 before, /device:TPU:18 now
where the time goes in v1:
time: 175 us; the launch traced here: 174 us
  Pallas kernels  114 us (65%)
  blocking collectives  38 us (22%)
  starting transfers between devices  15.3 us (9%)
  local copies, waits for them, and re-layouts  6.78 us (4%)
    pallas_call x1, Pallas kernels, body(): pl.pallas_call(near_kernel, out_shape=jax.ShapeDtypeStruct((rhs, cells),...  91.2 us
    all_gather x1, blocking collectives, body(): roots = lax.all_gather(table[rows - 1:], 'dev', axis=0, tiled=True)  38 us
    pallas_call x1, Pallas kernels, body(): pl.pallas_call(down_kernel, out_shape=jax.ShapeDtypeStruct((rhs, cells),...  17.6 us
    pallas_call x1, Pallas kernels, body(): pl.pallas_call(up_kernel, out_shape=jax.ShapeDtypeStruct((rows, rhs, 2 *...  5.26 us
    unnamed x18, local copies, waits for them, and re-layouts  4.1 us
  transfers between devices with their start and end apart: 6, of which 0 were waited for; matrix products, arithmetic and copies ran while one was open for 2% of the time, Pallas kernels for 55%

profile of v1, /device:TPU:18, one launch (start us, length us, event | category | flops | bytes accessed | tf_op | source)
XLA Modules:
  0.0 174.3 jit_solution(10857808227393487217)
XLA Ops:
  0.0 1.0 fusion.1
  1.0 1.9 %collective-permute-start.1 = (f32[3,8192]{1,0:T(4,128)S(1)}, f32[3,8192]{1,0:T(4,128)S(1)}, u32[]{:S(2)}, u32[]{:S(2)}) collective-permute-start(f32[3,8192]{1,0:T(4,128)S(1)} %get-tuple-element.7), channel_id=1, source_target_pairs={{1,0},{2,1},{3,2},{4,3},{5,4},{6,5},{7,6},{8,7},{9,8},{10,9},{11,1... | collective-permute-start | bytes 294920 | tf_op jit(solution)/shard_map/ppermute | solution.py:342
  2.9 2.4 %collective-permute-start = (f32[3,8192]{1,0:T(4,128)S(1)}, f32[3,8192]{1,0:T(4,128)S(1)}, u32[]{:S(2)}, u32[]{:S(2)}) collective-permute-start(f32[3,8192]{1,0:T(4,128)S(1)} %get-tuple-element.8), channel_id=1, source_target_pairs={{0,1},{1,2},{2,3},{3,4},{4,5},{5,6},{6,7},{7,8},{8,9},{9,10},{10,1... | collective-permute-start | bytes 294920 | tf_op jit(solution)/shard_map/ppermute | solution.py:341
  5.4 1.0 fusion
  6.4 3.2 %collective-permute-start.3 = (bf16[8,8192]{1,0:T(8,128)(2,1)S(1)}, bf16[8,8192]{1,0:T(8,128)(2,1)S(1)}, u32[]{:S(2)}, u32[]{:S(2)}) collective-permute-start(bf16[8,8192]{1,0:T(8,128)(2,1)S(1)} %get-tuple-element.5), channel_id=1, source_target_pairs={{1,0},{2,1},{3,2},{4,3},{5,4},{6,5},{7,6},{8,7},{9,8},{10,9},{11,1... | collective-permute-start | bytes 393224 | tf_op jit(solution)/shard_map/ppermute | solution.py:344
  9.5 0.0 copy-start
  9.5 0.0 copy-start.1
  9.5 2.6 %collective-permute-start.2 = (bf16[8,8192]{1,0:T(8,128)(2,1)S(1)}, bf16[8,8192]{1,0:T(8,128)(2,1)S(1)}, u32[]{:S(2)}, u32[]{:S(2)}) collective-permute-start(bf16[8,8192]{1,0:T(8,128)(2,1)S(1)} %get-tuple-element.6), channel_id=1, source_target_pairs={{0,1},{1,2},{2,3},{3,4},{4,5},{5,6},{6,7},{7,8},{8,9},{9,10},{10,1... | collective-permute-start | bytes 393224 | tf_op jit(solution)/shard_map/ppermute | solution.py:343
  12.2 5.3 %upward.1.own_ref = f32[63,8,128]{2,1,0:T(8,128)} custom-call(bf16[8,16384]{1,0:T(8,128)(2,1)} %vec_ref.3, bf16[64,64,256]{2,1,0:T(8,128)(2,1)} %basis_ref.3, bf16[63,64,128]{2,1,0:T(8,128)(2,1)} %transfer_ref.3, f32[63,192]{1,0:T(8,128)} %skeleton_ref.1), custom_call_target="tpu_custom_call" | custom-call | flops 2147483648 | bytes 4194304 | tf_op jit(solution)/shard_map/upward/pallas_call | solution.py:346
  17.4 2.9 %collective-permute-start.5 = (f32[63,8,128]{2,1,0:T(8,128)}, f32[63,8,128]{2,1,0:T(8,128)S(1)}, u32[]{:S(2)}, u32[]{:S(2)}) collective-permute-start(f32[63,8,128]{2,1,0:T(8,128)} %upward.1.own_ref), channel_id=1, source_target_pairs={{1,0},{2,1},{3,2},{4,3},{5,4},{6,5},{7,6},{8,7},{9,8},{10,9},{11,1... | collective-permute-start | bytes 774152 | tf_op jit(solution)/shard_map/ppermute | solution.py:360
  20.4 0.7 slice.20
  21.0 0.7 copy.12.list_ref
  21.7 0.7 copy.13.far_ref
  22.4 38.0 %all_gather.3.roots_ref = f32[32,8,128]{2,1,0:T(8,128)} all-gather(f32[1,8,128]{2,1,0:T(8,128)S(1)} %slice.20), channel_id=1, replica_groups=mesh['dev'=32] {'dev'}, dimensions={0}, use_global_device_ids=true | all-gather | bytes 135168 | tf_op jit(solution)/shard_map/all_gather | solution.py:361
  60.4 2.2 %collective-permute-start.4 = (f32[63,8,128]{2,1,0:T(8,128)}, f32[63,8,128]{2,1,0:T(8,128)S(1)}, u32[]{:S(2)}, u32[]{:S(2)}) collective-permute-start(f32[63,8,128]{2,1,0:T(8,128)} %upward.1.own_ref), channel_id=1, source_target_pairs={{0,1},{1,2},{2,3},{3,4},{4,5},{5,6},{6,7},{7,8},{8,9},{9,10},{10,1... | collective-permute-start | bytes 774152 | tf_op jit(solution)/shard_map/ppermute | solution.py:359
  62.7 0.0 copy-start.5
  62.7 0.0 collective-permute-done.3.vec_right_ref
  62.7 0.6 copy-done.5
  63.3 0.0 copy-done.6
  63.4 0.7 copy-done.7
  64.0 91.2 %near.1.near_ref = f32[8,16384]{1,0:T(8,128)} custom-call(s32[64,8]{1,0:T(8,128)} %copy.12.list_ref, f32[3,16384]{1,0:T(4,128)} %points_ref.1, f32[3,8192]{1,0:T(4,128)} %copy-done.5, f32[3,8192]{1,0:T(4,128)} %copy-done.4, bf16[8,16384]{1,0:T(8,128)(2,1)} %vec_ref.3, bf16[8,8192]{1,0:T(8,128)(2,1)} %copy-done.7, bf16[8,8192]{1,0:T(8,128)(2,1)} %copy-done.6), custom_call_target="tpu_custom_call" | custom-call | flops 42949672960 | bytes 2097152 | tf_op jit(solution)/shard_map/near/pallas_call | solution.py:364
  155.3 0.7 copy-done.2
  156.0 0.7 copy-done.3
  156.7 17.6 %downward.1 = f32[8,16384]{1,0:T(8,128)} custom-call(s32[62,4]{1,0:T(8,128)} %copy.13.far_ref, f32[8,16384]{1,0:T(8,128)} %near.1.near_ref, bf16[64,64,256]{2,1,0:T(8,128)(2,1)} %basis_ref.3, bf16[63,64,128]{2,1,0:T(8,128)(2,1)} %transfer_ref.3, f32[63,8,128]{2,1,0:T(8,128)} %upward.1.own_ref, f32[63,8,128]{2,1,0:T(8,128)} %copy-done.3, ...), custom_call_target="tpu_custom_call" | custom-call | flops 2147483648 | bytes 4194304 | tf_op jit(solution)/shard_map/downward/pallas_call | solution.py:383
  (13 shorter events, 0.0 us)
Async XLA Ops:
  1.0 59.4 %collective-permute-start.1 = (f32[3,8192]{1,0:T(4,128)S(1)}, f32[3,8192]{1,0:T(4,128)S(1)}, u32[]{:S(2)}, u32[]{:S(2)}) collective-permute-start(f32[3,8192]{1,0:T(4,128)S(1)} %get-tuple-element.7), channel_id=1, source_target_pairs={{1,0},{2,1},{3,2},{4,3},{5,4},{6,5},{7,6},{8,7},{9,8},{10,9},{11,1... | collective-permute-start | bytes 294920 | tf_op jit(solution)/shard_map/ppermute | solution.py:342
  2.9 59.7 %collective-permute-start = (f32[3,8192]{1,0:T(4,128)S(1)}, f32[3,8192]{1,0:T(4,128)S(1)}, u32[]{:S(2)}, u32[]{:S(2)}) collective-permute-start(f32[3,8192]{1,0:T(4,128)S(1)} %get-tuple-element.8), channel_id=1, source_target_pairs={{0,1},{1,2},{2,3},{3,4},{4,5},{5,6},{6,7},{7,8},{8,9},{9,10},{10,1... | collective-permute-start | bytes 294920 | tf_op jit(solution)/shard_map/ppermute | solution.py:341
  6.4 56.3 %collective-permute-start.3 = (bf16[8,8192]{1,0:T(8,128)(2,1)S(1)}, bf16[8,8192]{1,0:T(8,128)(2,1)S(1)}, u32[]{:S(2)}, u32[]{:S(2)}) collective-permute-start(bf16[8,8192]{1,0:T(8,128)(2,1)S(1)} %get-tuple-element.5), channel_id=1, source_target_pairs={{1,0},{2,1},{3,2},{4,3},{5,4},{6,5},{7,6},{8,7},{9,8},{10,9},{11,1... | collective-permute-start | bytes 393224 | tf_op jit(solution)/shard_map/ppermute | solution.py:344
  9.5 11.5 %copy-start = (s32[64,8]{0,1:T(8,128)S(1)}, s32[64,8]{0,1:T(8,128)}, u32[]{:S(2)}) copy-start(s32[64,8]{0,1:T(8,128)} %param.12) | copy-start | bytes 6148
  9.5 12.2 %copy-start.1 = (s32[62,4]{0,1:T(4,128)S(1)}, s32[62,4]{0,1:T(4,128)}, u32[]{:S(2)}) copy-start(s32[62,4]{0,1:T(4,128)} %param.13) | copy-start | bytes 2980
  9.5 53.2 %collective-permute-start.2 = (bf16[8,8192]{1,0:T(8,128)(2,1)S(1)}, bf16[8,8192]{1,0:T(8,128)(2,1)S(1)}, u32[]{:S(2)}, u32[]{:S(2)}) collective-permute-start(bf16[8,8192]{1,0:T(8,128)(2,1)S(1)} %get-tuple-element.6), channel_id=1, source_target_pairs={{0,1},{1,2},{2,3},{3,4},{4,5},{5,6},{6,7},{7,8},{8,9},{9,10},{10,1... | collective-permute-start | bytes 393224 | tf_op jit(solution)/shard_map/ppermute | solution.py:343
  17.4 137.8 %collective-permute-start.5 = (f32[63,8,128]{2,1,0:T(8,128)}, f32[63,8,128]{2,1,0:T(8,128)S(1)}, u32[]{:S(2)}, u32[]{:S(2)}) collective-permute-start(f32[63,8,128]{2,1,0:T(8,128)} %upward.1.own_ref), channel_id=1, source_target_pairs={{1,0},{2,1},{3,2},{4,3},{5,4},{6,5},{7,6},{8,7},{9,8},{10,9},{11,1... | collective-permute-start | bytes 774152 | tf_op jit(solution)/shard_map/ppermute | solution.py:360
  60.4 2.3 %copy-start.4 = (f32[3,8192]{1,0:T(4,128)}, f32[3,8192]{1,0:T(4,128)S(1)}, u32[]{:S(2)}) copy-start(f32[3,8192]{1,0:T(4,128)S(1)} %collective-permute-done.1.points_right_ref) | copy-start | bytes 294916
  60.4 94.9 %collective-permute-start.4 = (f32[63,8,128]{2,1,0:T(8,128)}, f32[63,8,128]{2,1,0:T(8,128)S(1)}, u32[]{:S(2)}, u32[]{:S(2)}) collective-permute-start(f32[63,8,128]{2,1,0:T(8,128)} %upward.1.own_ref), channel_id=1, source_target_pairs={{0,1},{1,2},{2,3},{3,4},{4,5},{5,6},{6,7},{7,8},{8,9},{9,10},{10,1... | collective-permute-start | bytes 774152 | tf_op jit(solution)/shard_map/ppermute | solution.py:359
  62.7 0.7 copy-start.5
  62.7 0.7 copy-start.6
  63.4 0.7 copy-start.7
  155.3 0.7 copy-start.2
  156.0 0.7 copy-start.3

commit v2 on v1

--- a/solution.py
+++ b/solution.py
@@ -1,4 +1,3 @@
-import functools
 import math
 
 import jax
@@ -14,15 +13,9 @@
 TINY = 1e-30
 FEATURES = 48
 GROUP = 4
+STRIP = 128
+MESH = pl.DeviceIdType.MESH
 VMEM_BYTES = 56 * 1024 * 1024
-
-
-def neighbours(cells):
-    count = lax.axis_size("dev")
-    ends = count - 1
-    from_left = lax.ppermute(cells, "dev", [(i, i + 1) for i in range(ends)])
-    from_right = lax.ppermute(cells, "dev", [(i + 1, i) for i in range(ends)])
-    return from_left, from_right
 
 
 def loop(count, unroll, step):
@@ -93,9 +86,64 @@
     return jnp.concatenate(parts + [jnp.zeros((5, rank), F32)], axis=0)
 
 
-def up_kernel(vec_ref, basis_ref, transfer_ref, skeleton_ref, table_ref, pair_ref):
+def up_kernel(
+    points_ref,
+    vec_ref,
+    basis_ref,
+    transfer_ref,
+    skeleton_ref,
+    table_ref,
+    table_left_ref,
+    table_right_ref,
+    roots_ref,
+    points_left_ref,
+    points_right_ref,
+    vec_left_ref,
+    vec_right_ref,
+    pair_ref,
+    send_sem,
+    recv_sem,
+    root_send_sem,
+    root_recv_sem,
+    own_sem,
+):
     leaf_dev, rank, leaf = basis_ref.shape
     local = leaf_dev.bit_length() - 1
+    rows = leaf_dev - 1
+    devices = roots_ref.shape[0]
+    me = lax.axis_index("dev")
+    right = (me + 1) % devices
+    left = (me + devices - 1) % devices
+
+    barrier = pltpu.get_barrier_semaphore()
+
+    def greet(shift, carry):
+        pl.semaphore_signal(
+            barrier, inc=1, device_id=((me + shift) % devices,), device_id_type=MESH
+        )
+        return carry
+
+    lax.fori_loop(1, devices, greet, 0)
+    pl.semaphore_wait(barrier, devices - 1)
+
+    def beside(source, arrival, device, index):
+        return pltpu.make_async_remote_copy(
+            src_ref=source,
+            dst_ref=arrival,
+            send_sem=send_sem.at[index],
+            recv_sem=recv_sem.at[index],
+            device_id=(device,),
+            device_id_type=MESH,
+        )
+
+    leaf_copies = [
+        beside(points_ref, points_left_ref, right, 0),
+        beside(points_ref, points_right_ref, left, 1),
+        beside(vec_ref, vec_left_ref, right, 2),
+        beside(vec_ref, vec_right_ref, left, 3),
+    ]
+    for copy in leaf_copies:
+        copy.start()
 
     def leaf_pair(pair):
         halves = []
@@ -119,6 +167,41 @@
             jnp.concatenate(coefs[2 * spot : 2 * spot + 2], axis=1)
             for spot in range(len(coefs) // 2)
         ]
+
+    root = table_ref.at[pl.ds(rows - 1, 1)]
+    mine = roots_ref.at[pl.ds(me, 1)]
+
+    def root_copy(shift):
+        return pltpu.make_async_remote_copy(
+            src_ref=root,
+            dst_ref=mine,
+            send_sem=root_send_sem.at[shift],
+            recv_sem=root_recv_sem.at[shift],
+            device_id=((me + shift) % devices,),
+            device_id_type=MESH,
+        )
+
+    def send_root(shift, carry):
+        root_copy(shift).start()
+        return carry
+
+    def wait_root(shift, carry):
+        root_copy(shift).wait()
+        return carry
+
+    table_copies = [
+        beside(table_ref, table_left_ref, right, 4),
+        beside(table_ref, table_right_ref, left, 5),
+    ]
+    for copy in table_copies:
+        copy.start()
+    lax.fori_loop(1, devices, send_root, 0)
+    own_copy = pltpu.make_async_copy(root, mine, own_sem)
+    own_copy.start()
+    for copy in leaf_copies + table_copies:
+        copy.wait()
+    lax.fori_loop(1, devices, wait_root, 0)
+    own_copy.wait()
 
 
 def near_kernel(
@@ -136,7 +219,7 @@
     task_target_ref,
     task_source_ref,
 ):
-    leaf_dev, slots = list_ref.shape
+    slots, leaf_dev = list_ref.shape
     leaf = points_ref.shape[1] // leaf_dev
     reach = leaf_dev // 2
     wide = leaf_dev + 2 * reach
@@ -146,10 +229,10 @@
         part = ref[:, pl.ds(start, chunk)]
         return jnp.concatenate([part, jnp.zeros((5, chunk), F32)], axis=0)
 
-    def fill(points, vecs, base, own):
+    def fill(points, vecs, base, first, length, own):
         def step(index):
-            start = pl.multiple_of(index * chunk, chunk)
-            spot = pl.multiple_of(base + start, chunk)
+            start = pl.multiple_of(first + index * chunk, chunk)
+            spot = pl.multiple_of(base + index * chunk, chunk)
             sources, targets = distance_factors(cells_of(points, start))
             source_ref[:, pl.ds(spot, chunk)] = sources
             if own:
@@ -157,18 +240,20 @@
                 out_ref[:, pl.ds(start, chunk)] = jnp.zeros((out_ref.shape[0], chunk), F32)
             wide_vec_ref[:, pl.ds(spot, chunk)] = vecs[:, pl.ds(start, chunk)].astype(F32)
 
-        loop(points.shape[1] // chunk, 2, step)
-
-    fill(points_left_ref, vec_left_ref, 0, False)
-    fill(points_ref, vec_ref, reach * leaf, True)
-    fill(points_right_ref, vec_right_ref, (reach + leaf_dev) * leaf, False)
+        loop(length // chunk, 2, step)
+
+    edge = reach * leaf
+    cells = leaf_dev * leaf
+    fill(points_left_ref, vec_left_ref, 0, cells - edge, edge, False)
+    fill(points_ref, vec_ref, edge, 0, cells, True)
+    fill(points_right_ref, vec_right_ref, edge + cells, 0, edge, False)
     empty = pl.ds(wide * leaf, leaf)
     source_ref[:, empty] = jnp.zeros((FEATURES, leaf), BF16)
     wide_vec_ref[:, empty] = jnp.zeros((wide_vec_ref.shape[0], leaf), F32)
 
     def enlist(target, count):
         for slot in range(slots):
-            offset = list_ref[target, slot]
+            offset = list_ref[slot, target]
             task_target_ref[count] = target
             task_source_ref[count] = target + offset + reach
             if slot == 0:
@@ -187,10 +272,15 @@
         for part in range(GROUP):
             target = pl.multiple_of(task_target_ref[index * GROUP + part] * leaf, leaf)
             source = pl.multiple_of(task_source_ref[index * GROUP + part] * leaf, leaf)
-            squares = product_rows(
-                source_ref[:, pl.ds(source, leaf)], target_ref[:, pl.ds(target, leaf)]
+            sources = source_ref[:, pl.ds(source, leaf)]
+            targets = target_ref[:, pl.ds(target, leaf)]
+            tile = jnp.concatenate(
+                [
+                    decay(product_rows(sources[:, start : start + STRIP], targets)).astype(BF16)
+                    for start in range(0, leaf, STRIP)
+                ],
+                axis=0,
             )
-            tile = decay(squares).astype(BF16)
             vec = wide_vec_ref[:, pl.ds(source, leaf)].astype(BF16)
             results.append((target, product(vec, tile)))
         for target, result in results:
@@ -271,8 +361,8 @@
             for part in range(2):
                 spot = pair * 2 + part
                 partners, weights = [], []
-                for slot in range(far_ref.shape[1]):
-                    offset = far_ref[first + spot, slot]
+                for slot in range(far_ref.shape[0]):
+                    offset = far_ref[slot, first + spot]
                     partner = spot + offset
                     side = jnp.where(partner < 0, 0, jnp.where(partner < count, 1, 2))
                     partners.append(wide_ref[side * rows + first + partner - (side - 1) * count])
@@ -281,7 +371,7 @@
                 halves.append(couple(mine[:, rank:], partners, weights))
             coupled_ref[first // 2 + pair] = jnp.concatenate(halves, axis=1)
 
-        loop(count // 2, 2, couple_pair)
+        loop(count // 2, 4, couple_pair)
 
     field = None
     for step in range(top - 1, -1, -1):
@@ -327,38 +417,55 @@
     leaf_dev, rank, leaf = leaf_basis.shape
     slots = near_list.shape[1]
     devices = lax.axis_size("dev")
-    reach = leaf_dev // 2
-    wide = leaf_dev + 2 * reach
+    wide = 2 * leaf_dev
     rows = leaf_dev - 1
-    edge = reach * leaf
     vmem = pl.BlockSpec(memory_space=pltpu.VMEM)
     smem = pl.BlockSpec(memory_space=pltpu.SMEM)
+    hbm = pl.BlockSpec(memory_space=pl.ANY)
     params = pltpu.CompilerParams(vmem_limit_bytes=VMEM_BYTES)
 
-    ends = devices - 1
-    to_right = [(i, i + 1) for i in range(ends)]
-    to_left = [(i + 1, i) for i in range(ends)]
-    points_left = lax.ppermute(points[:, cells - edge :], "dev", to_right)
-    points_right = lax.ppermute(points[:, :edge], "dev", to_left)
-    vec_left = lax.ppermute(vectors[:, cells - edge :], "dev", to_right)
-    vec_right = lax.ppermute(vectors[:, :edge], "dev", to_left)
-
-    table = pl.pallas_call(
+    table_shape = jax.ShapeDtypeStruct((rows, rhs, 2 * rank), F32)
+    points_shape = jax.ShapeDtypeStruct(points.shape, points.dtype)
+    vec_shape = jax.ShapeDtypeStruct(vectors.shape, vectors.dtype)
+    (
+        table,
+        table_left,
+        table_right,
+        roots,
+        points_left,
+        points_right,
+        vec_left,
+        vec_right,
+    ) = pl.pallas_call(
         up_kernel,
-        out_shape=jax.ShapeDtypeStruct((rows, rhs, 2 * rank), F32),
-        in_specs=[vmem] * 4,
-        out_specs=vmem,
-        scratch_shapes=[pltpu.VMEM((leaf_dev // 2, rhs, 2 * rank), F32)],
-        compiler_params=params,
+        out_shape=(
+            table_shape,
+            table_shape,
+            table_shape,
+            jax.ShapeDtypeStruct((devices, rhs, 2 * rank), F32),
+            points_shape,
+            points_shape,
+            vec_shape,
+            vec_shape,
+        ),
+        in_specs=[vmem] * 5,
+        out_specs=(vmem,) + (hbm,) * 7,
+        scratch_shapes=[
+            pltpu.VMEM((leaf_dev // 2, rhs, 2 * rank), F32),
+            pltpu.SemaphoreType.DMA((6,)),
+            pltpu.SemaphoreType.DMA((6,)),
+            pltpu.SemaphoreType.DMA((devices,)),
+            pltpu.SemaphoreType.DMA((devices,)),
+            pltpu.SemaphoreType.DMA,
+        ],
+        compiler_params=pltpu.CompilerParams(
+            vmem_limit_bytes=VMEM_BYTES, collective_id=0, has_side_effects=True
+        ),
         cost_estimate=pl.CostEstimate(
             flops=2 * 256 * 256 * 256 * 64, bytes_accessed=4 * 2**20, transcendentals=0
         ),
         name="upward",
-    )(vectors, leaf_basis, transfer, skeleton)
-
-    table_left = lax.ppermute(table, "dev", to_right)
-    table_right = lax.ppermute(table, "dev", to_left)
-    roots = lax.all_gather(table[rows - 1 :], "dev", axis=0, tiled=True)
+    )(points, vectors, leaf_basis, transfer, skeleton)
 
     tasks = leaf_dev * slots + 2 * GROUP
     near = pl.pallas_call(
@@ -378,7 +485,7 @@
             flops=2 * 256 * 256 * 256 * 64 * 20, bytes_accessed=2 * 2**20, transcendentals=2**25
         ),
         name="near",
-    )(near_list, points, points_left, points_right, vectors, vec_left, vec_right)
+    )(near_list.T, points, points_left, points_right, vectors, vec_left, vec_right)
 
     return pl.pallas_call(
         down_kernel,
@@ -397,7 +504,7 @@
         ),
         name="downward",
     )(
-        far_list,
+        far_list.T,
         near,
         leaf_basis,
         transfer,

time: 175 us -> 126 us (0.72)
  the two profiles are of different devices: /device:TPU:18 before, /device:TPU:5 now
where the time goes in v2:
time: 126 us; the launch traced here: 123 us
  Pallas kernels  123 us (98%)
    pallas_call x1, Pallas kernels, body(): pl.pallas_call(near_kernel, out_shape=jax.ShapeDtypeStruct((rhs, cells),...  80.1 us
    pallas_call x1, Pallas kernels, body(): pl.pallas_call(up_kernel, out_shape=(table_shape, table_shape, table_shap...  29.1 us
    pallas_call x1, Pallas kernels, body(): pl.pallas_call(down_kernel, out_shape=jax.ShapeDtypeStruct((rhs, cells),...  14.3 us

profile of v2, /device:TPU:5, one launch (start us, length us, event | category | flops | bytes accessed | tf_op | source)
XLA Modules:
  0.0 123.4 jit_solution(1644933234747584910)
XLA Ops:
  0.0 29.1 %upward.1 = (f32[63,8,128]{2,1,0:T(8,128)}, f32[63,8,128]{2,1,0:T(8,128)}, f32[63,8,128]{2,1,0:T(8,128)}, f32[32,8,128]{2,1,0:T(8,128)}, f32[3,16384]{1,0:T(4,12...) custom-call(f32[3,16384]{1,0:T(4,128)} %points_ref.3, bf16[8,16384]{1,0:T(8,128)(2,1)} %vec_ref.3, ...), custom_call_target="tpu_custom_call" | custom-call | flops 2147483648 | bytes 4194304 | tf_op jit(solution)/shard_map/upward/pallas_call | solution.py:439
  29.1 80.1 %near.1.near_ref = f32[8,16384]{1,0:T(8,128)} custom-call(s32[8,64]{1,0:T(8,128)} %bitcast.2, f32[3,16384]{1,0:T(4,128)} %points_ref.3, f32[3,16384]{1,0:T(4,128)} %get-tuple-element.13.points_left_ref, f32[3,16384]{1,0:T(4,128)} %get-tuple-element.14.points_right_ref, bf16[8,16384]{1,0:T(8,128)(2,1)} %vec_ref.3, ...), custom_call_target="tpu_custom_call" | custom-call | flops 42949672960 | bytes 2097152 | tf_op jit(solution)/shard_map/near/pallas_call | solution.py:471
  109.2 14.3 %downward.1 = f32[8,16384]{1,0:T(8,128)} custom-call(s32[4,62]{1,0:T(4,128)} %bitcast.3, f32[8,16384]{1,0:T(8,128)} %near.1.near_ref, bf16[64,64,256]{2,1,0:T(8,128)(2,1)} %basis_ref.3, bf16[63,64,128]{2,1,0:T(8,128)(2,1)} %transfer_ref.3, f32[63,8,128]{2,1,0:T(8,128)} %get-tuple-element.17.own_ref, f32[63,8,128]{2,1,0:T(8,128)} %get-tuple-element.18.left_ref, ...), custom_call_target="tpu_custom_call" | custom-call | flops 2147483648 | bytes 4194304 | tf_op jit(solution)/shard_map/downward/pallas_call | solution.py:490
